TPU v7x, 512 devices: a whole 4x4x16 slice. The times are simulated.
512 devices in a mesh: replica: 32 (over z, y_hi), tensor: 16 (over y_lo, x, core).
Axes of the slice: x: 4, y: 4 (y_hi: 2, y_lo: 2; y = y_hi * 2 + y_lo), z: 16, core: 2. Of those that a mesh axis runs over, the one named last changes fastest.
Arguments:
- key_head_weight: bfloat16 [16, 128, 8192], P('tensor'), may hold values from -6 to 6
- down_factor_slots: float32 [32, 2, 8192], P('replica', None, 'tensor'), may hold values from -6 to 6
- adapter_up_factor: float32 [64, 1024], P('replica'), may hold values from -0.2 to 0.2
- piece_slot_index: int32 [32], replicated, may hold values from 0 to 31, each once
Outputs:
- merged: bfloat16 [16, 128, 8192], P('tensor')
Inputs may be any that keep to these rules, and one draw needn't show every extreme that they name: Piece p lies in slot piece_slot_index[p] of down_factor_slots; every slot holds exactly one piece.
All inputs are finite; a program needn't handle non-finite values.
Results may differ from a plain program's by a relative error of at most 0.001.
Values sent between devices are 32-bit elements; how exact they have to be, the bound alone decides.
A program may use at most 64 MiB of HBM per device.

v0:
```python
import jax
import jax.numpy as jnp
from jax import lax
from jax.sharding import PartitionSpec as P

KV_HEADS = 8


merge_scale = 2.0


def arrange_pieces(slot_row_count, piece_slot_index, factor_rank):
    ordered = jnp.take(slot_row_count, piece_slot_index, axis=0)
    return ordered.reshape(factor_rank, ordered.shape[-1])


def merge_weight_block(resident_block, down_factor_rows, adapter_rows):
    lowrank_update = jnp.dot(
        adapter_rows.T,
        down_factor_rows,
        preferred_element_type=jnp.float32,
        precision=lax.Precision.HIGHEST,
    )
    return (resident_block.astype(jnp.float32) + merge_scale * lowrank_update[None]).astype(
        jnp.bfloat16
    )


def local(key_head_weight, down_factor_slots, adapter_up_factor, piece_slot_index):
    output_units = key_head_weight.shape[1]
    copies = max(1, lax.axis_size("tensor") // KV_HEADS)
    first_index = lax.axis_index("tensor") // copies * output_units
    adapter_columns = lax.dynamic_slice_in_dim(adapter_up_factor, first_index, output_units, 1)
    owner_rows = lax.all_gather(down_factor_slots, "tensor", axis=2, tiled=True)
    slot_row_count, adapter_rows = (
        lax.all_gather(owner_rows, "replica", axis=0, tiled=True),
        lax.all_gather(adapter_columns, "replica", axis=0, tiled=True),
    )
    down_factor_rows = arrange_pieces(slot_row_count, piece_slot_index, adapter_rows.shape[0])
    return merge_weight_block(key_head_weight, down_factor_rows, adapter_rows)


def solution(mesh):
    in_specs = (P("tensor", None, None), P("replica", None, "tensor"), P("replica", None), P())
    out_specs = P("tensor", None, None)
    return jax.shard_map(local, mesh=mesh, in_specs=in_specs, out_specs=out_specs, check_vma=False)
```

profile of v0, /device:TPU:2, one launch (start us, length us, event | category | flops | bytes accessed | tf_op | source)
XLA Modules:
  0.0 201.6 jit_solution(13053699690656250366)
XLA Ops:
  6.5 0.0 copy-start
  6.5 0.0 all-gather.3.cloned.1.call-start
  6.5 23.7 %all_gather.10 = f32[1,2,8192]{2,1,0:T(2,128)} all-gather(f32[1,2,512]{2,1,0:T(2,128)} %param.5), channel_id=1, replica_groups=mesh['replica'=32,'tensor'=16] {'tensor'}, dimensions={2}, use_global_device_ids=true | all-gather | bytes 69632 | tf_op jit(solution)/shard_map/all_gather | solution.py:34
  30.3 0.0 all-gather.3.cloned.1.call-update
  30.3 0.7 compare_and_fusion
  31.0 0.1 broadcast_in_dim.17
  31.0 0.1 broadcast_in_dim.18
  31.2 0.0 copy-done
  31.2 77.4 %all-gather = f32[32,2,128]{2,1,0:T(2,128)S(1)} all-gather(f32[1,2,128]{2,1,0:T(2,128)S(1)} %dynamic-slice_bitcast_fusion), channel_id=1, replica_groups=mesh['replica'=32,'tensor'=16] {'replica'}, dimensions={0}, use_global_device_ids=true | all-gather | bytes 33792 | tf_op jit(solution)/shard_map/all_gather | solution.py:37
  108.6 0.7 compare_select_fusion
  109.2 70.9 %all-gather.3.cloned.1.call-done = f32[32,2,8192]{2,1,0:T(2,128)} async-done(((f32[1,2,8192]{2,1,0:T(2,128)}), f32[32,2,8192]{2,1,0:T(2,128)}) %all-gather.3.cloned.1.call-update) | async-done | bytes 2097168 | tf_op jit(solution)/shard_map/all_gather | solution.py:36
  180.2 5.6 %gather_fusion = f32[32,2,8192]{2,1,0:T(2,128)} fusion(f32[32,2,8192]{2,1,0:T(2,128)} %all-gather.3.cloned.1.call-done, s32[1024]{0:T(1024)S(1)} %pad_clamp_fusion), kind=kCustom, calls=%fused_computation | custom fusion | bytes 4194432 | tf_op jit(solution)/shard_map/jit(_take)/gather | solution.py:13
  185.7 2.7 %gather.7 = f32[64,8192]{1,0:T(8,128)S(1)} reshape(f32[32,2,8192]{2,1,0:T(2,128)} %gather_fusion) | data formatting | bytes 4194304 | tf_op jit(solution)/shard_map/jit(_take)/gather | solution.py:13
  188.4 6.4 %fusion.2 = bf16[1,128,8192]{2,1,0:T(8,128)(2,1)} fusion(f32[64,128]{1,0:T(8,128)S(1)} %bitcast.10, bf16[1,128,8192]{2,1,0:T(8,128)(2,1)} %param.4, f32[64,8192]{1,0:T(8,128)S(1)} %gather.7, pred[64]{0:T(512)(128)(4,1)S(1)} %broadcast_in_dim.18), kind=kOutput, calls=%fused_computation.4 | convolution fusion | flops 810024960 | bytes 6324288 | tf_op jit(solution)/shard_map/dot_general | solution.py:18
  (2 shorter events, 0.0 us)
Async XLA Ops:
  6.5 24.6 %copy-start = (f32[2,1024]{1,0:T(2,128)S(1)}, f32[2,1024]{1,0:T(2,128)}, u32[]{:S(2)}) copy-start(f32[2,1024]{1,0:T(2,128)} %param.6) | copy-start | bytes 24580
  6.5 173.6 %all-gather.3.cloned.1.call-start = ((), (), s32[]{:S(2)}) async-start(), calls=%async_computation | async-start | bytes 2162688 | tf_op jit(solution)/shard_map/all_gather | solution.py:36
Sparse Core Ops, SparseCore 0:
  30.4 149.7 all-gather.2
where the time goes:
time: 202 us
  blocking collectives  101 us (50%)
  waiting for transfers between devices  70.9 us (35%)
  between operations  13.4 us (7%)
  local copies, waits for them, and re-layouts  8.46 us (4%)
  matrix products  6.37 us (3%)
    all_gather x1, blocking collectives, local(): lax.all_gather(adapter_columns, 'replica', axis=0, tiled=True)  77.4 us
    all_gather x1, waiting for transfers between devices, local(): lax.all_gather(owner_rows, 'replica', axis=0, tiled=True)  70.9 us
    all_gather x1, blocking collectives, local(): owner_rows = lax.all_gather(down_factor_slots, 'tensor', axis=2, tiled=True)  23.7 us
    gather x2, local copies, waits for them, and re-layouts, arrange_pieces(): ordered = jnp.take(slot_row_count, piece_slot_index, axis=0)  8.26 us
    dot_general x1, matrix products, merge_weight_block(): jnp.dot(adapter_rows.T, down_factor_rows, preferred_element_type=jnp.floa...  6.37 us
  transfers between devices with their start and end apart: 1, of which 1 were waited for; matrix products, arithmetic and copies ran while one was open for 1% of the time, Pallas kernels for 0%

commit v1 on v0

v1 whole, which is shorter than its diff:
```python
import jax
import jax.numpy as jnp
from jax import lax
from jax.experimental import pallas as pl
from jax.experimental.pallas import tpu as pltpu
from jax.sharding import PartitionSpec as P

MESH = pl.DeviceIdType.MESH
MERGE_SCALE = 2.0
NX, NY, NZ = 4, 4, 16
LANES = 128
COLUMNS = 512


def place(x, y, z, core):
    return (z * 2 + y // 2, ((y % 2) * NX + x) * 2 + core)


def block_of(x, y, core):
    return (x * NY + y) * 2 + core


def kernel(index_ref, down_ref, up_ref, weight_ref, out_ref, index, tiles, ups, weight, left,
           weight_sem, small_sem, z_send, z_recv, up_send, up_recv, up_pair_send, up_pair_recv,
           xy_send, xy_recv, core_send):
    replica, tensor = lax.axis_index("replica"), lax.axis_index("tensor")
    z, y_hi = replica // 2, replica % 2
    y, x, core = y_hi * 2 + tensor // 8, (tensor // 2) % NX, tensor % 2
    mine = block_of(x, y, core)
    head = tensor // 2

    z_others = []
    for k in range(8, 0, -1):
        z_others.append(lax.rem(z + k, NZ))
        if k < 8:
            z_others.append(lax.rem(z + NZ - k, NZ))
    plane = [((x + dx) % NX, (y + dy) % NY)
             for dx, dy in [(2, 2), (2, 1), (2, 3), (1, 2), (3, 2), (1, 1), (1, 3), (3, 1), (3, 3),
                            (2, 0), (0, 2), (1, 0), (3, 0), (0, 1), (0, 3)]]

    barrier = pltpu.get_barrier_semaphore()
    for other in z_others:
        pl.semaphore_signal(barrier, inc=1, device_id=place(x, y, other, core), device_id_type=MESH)
    for a, b in plane:
        pl.semaphore_signal(barrier, inc=1, device_id=place(a, b, z, core), device_id_type=MESH)
    pl.semaphore_signal(barrier, inc=1, device_id=place(x, y, z, 1 - core), device_id_type=MESH)

    own_tile = pltpu.make_async_copy(down_ref, tiles.at[mine, z], small_sem.at[0])
    own_up = pltpu.make_async_copy(
        up_ref.at[:, pl.ds(pl.multiple_of(head * LANES, LANES), LANES)], ups.at[y_hi, z], small_sem.at[1])
    get_index = pltpu.make_async_copy(index_ref, index, small_sem.at[2])
    get_weight = pltpu.make_async_copy(weight_ref, weight, weight_sem)
    own_tile.start()
    own_up.start()
    get_index.start()
    get_weight.start()
    own_tile.wait()
    own_up.wait()

    pl.semaphore_wait(barrier, len(z_others) + len(plane) + 1)

    def send(ref, send_sem, recv_sem, where):
        pltpu.make_async_remote_copy(src_ref=ref, dst_ref=ref, send_sem=send_sem, recv_sem=recv_sem,
                                     device_id=where, device_id_type=MESH).start()

    def wait(ref, sem):
        pltpu.make_async_copy(ref, ref, sem).wait()

    for other in z_others:
        send(tiles.at[mine, z], z_send, z_recv, place(x, y, other, core))
    for other in z_others:
        send(ups.at[y_hi, z], up_send, up_recv, place(x, y, other, core))

    wait(tiles.at[mine, pl.ds(0, NZ - 1)], z_recv)
    for a, b in plane:
        send(tiles.at[mine], xy_send, xy_recv.at[mine], place(a, b, z, core))
    send(tiles.at[mine], core_send, xy_recv.at[mine], place(x, y, z, 1 - core))
    wait(ups.at[y_hi, pl.ds(0, NZ - 1)], up_recv)
    send(ups.at[y_hi], up_pair_send, up_pair_recv, place(x, (y + 2) % NY, z, core))

    get_index.wait()
    wait(ups.at[y_hi], up_pair_recv)

    iota = lambda shape, dim: lax.broadcasted_iota(jnp.int32, shape, dim)
    k32 = iota((192, 32), 0) % 64
    slot = (k32 % 16) * 2 + k32 // 32
    holds = (index[...] == slot).astype(jnp.bfloat16)
    q = iota((32, 64), 1)
    spread = (iota((32, 64), 0) == ((q // 2) % 16) * 2 + q // 32).astype(jnp.bfloat16)
    k64, q64 = iota((192, 64), 0), iota((192, 64), 1)
    pick = jnp.dot(holds, spread, preferred_element_type=jnp.float32)
    pick = jnp.where(q64 % 2 == (k64 // 16) % 2, pick, 0.0)
    pick_high = jnp.where(k64 < 128, pick, 0.0).astype(jnp.bfloat16)
    pick_low = jnp.where(k64 < 128, 0.0, pick).astype(jnp.bfloat16)
    rows = MERGE_SCALE * ups[...].reshape(64, LANES)
    turned = rows.T
    high = turned.astype(jnp.bfloat16)
    low = (turned - high.astype(jnp.float32)).astype(jnp.bfloat16)
    nt = (((1,), (1,)), ((), ()))
    left[...] = (lax.dot_general(high, pick_high, nt, preferred_element_type=jnp.float32)
                 + lax.dot_general(low, pick_low, nt, preferred_element_type=jnp.float32)).astype(jnp.bfloat16)
    get_weight.wait()

    def merge(a, b_low, which):
        pair = [block_of(a, b_low, which), block_of(a, b_low + 2, which)]
        parts = []
        for c in range(4):
            parts.append(jnp.concatenate(
                [tiles[w, :, c * 2 + i, :] for w in pair for i in range(2)], axis=0))
        right = jnp.concatenate(parts, axis=1)
        right_high = right.astype(jnp.bfloat16)
        right_low = (right - right_high.astype(jnp.float32)).astype(jnp.bfloat16)
        right = jnp.concatenate([right_high, right_low, right_high], axis=0)
        update = jnp.dot(left[...], right, preferred_element_type=jnp.float32)
        at = pl.ds(pl.multiple_of(((b_low * NX + a) * 2 + which) * COLUMNS, COLUMNS), COLUMNS)
        out_ref[:, at] = (weight[:, at].astype(jnp.float32) + update).astype(jnp.bfloat16)

    def offsets(p):
        q = p // 2
        return q + (q // 2) * (1 - 2 * (q % 2)), p % 2

    def step(p, carry):
        dx, dy = offsets(p)
        a, b, b2 = (x + dx) % NX, (y + dy) % NY, (y + dy + 2) % NY
        first, second = block_of(a, b, core), block_of(a, b2, core)

        @pl.when(p > 0)
        def _():
            wait(tiles.at[first], xy_recv.at[first])
            send(tiles.at[first], core_send, xy_recv.at[first], place(x, y, z, 1 - core))

        wait(tiles.at[second], xy_recv.at[second])
        send(tiles.at[second], core_send, xy_recv.at[second], place(x, y, z, 1 - core))
        merge(a, b % 2, core)

        @pl.when(p > 0)
        def _():
            sibling(p - 1)

        return carry

    def sibling(p):
        dx, dy = offsets(p)
        a, b, b2 = (x + dx) % NX, (y + dy) % NY, (y + dy + 2) % NY
        for w in (block_of(a, b, 1 - core), block_of(a, b2, 1 - core)):
            wait(tiles.at[w], xy_recv.at[w])
        merge(a, b % 2, 1 - core)

    lax.fori_loop(0, 8, step, 0)
    sibling(7)

    wait(tiles.at[mine, pl.ds(0, NZ - 1)], z_send)
    wait(ups.at[y_hi, pl.ds(0, NZ - 1)], up_send)
    wait(ups.at[y_hi], up_pair_send)
    wait(tiles.at[pl.ds(0, 15)], xy_send)
    wait(tiles.at[pl.ds(0, 16)], core_send)


def local(key_head_weight, down_factor_slots, adapter_up_factor, piece_slot_index):
    units, width = key_head_weight.shape[1:]
    tile = down_factor_slots.reshape(2, 4, LANES).transpose(1, 0, 2).reshape(8, LANES)
    dma = pltpu.SemaphoreType.DMA
    merged = pl.pallas_call(
        kernel,
        out_shape=jax.ShapeDtypeStruct((units, width), jnp.bfloat16),
        in_specs=[pl.BlockSpec(memory_space=pltpu.HBM)] * 4,
        out_specs=pl.BlockSpec(memory_space=pltpu.VMEM),
        scratch_shapes=[
            pltpu.VMEM((1, 32), jnp.int32),
            pltpu.VMEM((32, NZ, 8, LANES), jnp.float32),
            pltpu.VMEM((2, NZ, 2, LANES), jnp.float32),
            pltpu.VMEM((units, width), jnp.bfloat16),
            pltpu.VMEM((units, 192), jnp.bfloat16),
            dma, dma((3,)), dma, dma, dma, dma, dma, dma, dma, dma((32,)), dma,
        ],
        compiler_params=pltpu.CompilerParams(
            collective_id=0, has_side_effects=True, vmem_limit_bytes=32 << 20),
        name="gather_and_merge",
    )(piece_slot_index.reshape(1, 32), tile, adapter_up_factor, key_head_weight.reshape(units, width))
    return merged.reshape(1, units, width)


def solution(mesh):
    in_specs = (P("tensor", None, None), P("replica", None, "tensor"), P("replica", None), P())
    out_specs = P("tensor", None, None)
    return jax.shard_map(local, mesh=mesh, in_specs=in_specs, out_specs=out_specs, check_vma=False)
```

time: 202 us -> 48.6 us (0.24)
  the two profiles are of different devices: /device:TPU:2 before, /device:TPU:1 now
where the time goes in v1:
time: 48.6 us; the launch traced here: 48.3 us
  Pallas kernels  43.4 us (89%)
  local copies, waits for them, and re-layouts  4.95 us (10%)
    pallas_call x1, Pallas kernels, local(): pl.pallas_call(kernel, out_shape=jax.ShapeDtypeStruct((units, width), jnp...  43.4 us
    unnamed x9, local copies, waits for them, and re-layouts  4.95 us

profile of v1, /device:TPU:1, one launch (start us, length us, event | category | flops | bytes accessed | tf_op | source)
XLA Modules:
  0.0 48.3 jit_solution(14860756483229869220)
XLA Ops:
  0.0 0.0 copy-start
  0.0 1.6 %copy-done = bf16[1,128,8192]{2,1,0:T(8,128)(2,1)S(1)} copy-done((bf16[1,128,8192]{2,1,0:T(8,128)(2,1)S(1)}, bf16[1,128,8192]{2,1,0:T(8,128)(2,1)}, u32[]{:S(2)}) %copy-start) | copy-done | bytes 2097176
  1.6 0.0 copy-start.1
  1.6 0.7 %copy-done.1 = f32[2,1024]{1,0:T(2,128)S(1)} copy-done((f32[2,1024]{1,0:T(2,128)S(1)}, f32[2,1024]{1,0:T(2,128)}, u32[]{:S(2)}) %copy-start.1) | copy-done | bytes 8216
  2.3 0.0 copy-start.2
  2.3 0.7 %copy-done.2 = f32[1,2,512]{2,1,0:T(2,128)S(1)} copy-done((f32[1,2,512]{2,1,0:T(2,128)S(1)}, f32[1,2,512]{2,1,0:T(2,128)}, u32[]{:S(2)}) %copy-start.2) | copy-done | bytes 4120
  3.0 0.0 copy-start.3
  3.0 0.7 %copy-done.3 = s32[32]{0:T(128)S(1)} copy-done((s32[32]{0:T(128)S(1)}, s32[32]{0:T(128)}, u32[]{:S(2)}) %copy-start.3) | copy-done | bytes 152
  3.6 43.4 %gather_and_merge.1 = bf16[128,8192]{1,0:T(8,128)(2,1)S(1)} custom-call(s32[1,32]{1,0:T(1,128)S(1)} %bitcast.11, f32[8,128]{1,0:T(8,128)S(1)} %bitcast.10, f32[2,1024]{1,0:T(2,128)S(1)} %copy-done.1, bf16[128,8192]{1,0:T(8,128)(2,1)S(1)} %bitcast.9), custom_call_target="tpu_custom_call" | custom-call | tf_op jit(solution)/shard_map/gather_and_merge/pallas_call | solution.py:163
  47.0 1.3 %copy.7 = bf16[1,128,8192]{2,1,0:T(8,128)(2,1)} copy(bf16[1,128,8192]{2,1,0:T(8,128)(2,1)S(1)} %bitcast.8) | data formatting | bytes 4194304
Async XLA Ops:
  0.0 1.6 %copy-start = (bf16[1,128,8192]{2,1,0:T(8,128)(2,1)S(1)}, bf16[1,128,8192]{2,1,0:T(8,128)(2,1)}, u32[]{:S(2)}) copy-start(bf16[1,128,8192]{2,1,0:T(8,128)(2,1)} %param.4) | copy-start | bytes 6291460
  1.6 0.7 %copy-start.1 = (f32[2,1024]{1,0:T(2,128)S(1)}, f32[2,1024]{1,0:T(2,128)}, u32[]{:S(2)}) copy-start(f32[2,1024]{1,0:T(2,128)} %up_ref.1) | copy-start | bytes 24580
  2.3 0.7 %copy-start.2 = (f32[1,2,512]{2,1,0:T(2,128)S(1)}, f32[1,2,512]{2,1,0:T(2,128)}, u32[]{:S(2)}) copy-start(f32[1,2,512]{2,1,0:T(2,128)} %param.5) | copy-start | bytes 12292
  3.0 0.7 %copy-start.3 = (s32[32]{0:T(128)S(1)}, s32[32]{0:T(128)}, u32[]{:S(2)}) copy-start(s32[32]{0:T(128)} %param.7) | copy-start | bytes 388

commit v2 on v1

v2 whole, which is shorter than its diff:
```python
import jax
import jax.numpy as jnp
from jax import lax
from jax.experimental import pallas as pl
from jax.experimental.pallas import tpu as pltpu
from jax.sharding import PartitionSpec as P

MESH = pl.DeviceIdType.MESH
MERGE_SCALE = 2.0
NX, NY, NZ = 4, 4, 16
CUBE = 4
HALF = 8
LANES = 128
COLUMNS = 512
PLANE = [(2, 2), (2, 1), (2, 3), (1, 2), (3, 2), (1, 1), (1, 3), (3, 1), (3, 3),
         (2, 0), (0, 2), (1, 0), (3, 0), (0, 1), (0, 3)]


def place(x, y, z, core):
    return (z * 2 + y // 2, ((y % 2) * NX + x) * 2 + core)


def block_of(x, y, core):
    return (core * NX + x) * NY + y


def exchanged(z):
    return z + CUBE * (z // HALF) * (1 - 2 * ((z // CUBE) % 2))


def kernel(index_ref, down_ref, up_ref, weight_ref, out_ref, index, tiles, ups, pair_up, weight, left,
           weight_sem, small_sem, z_send, z_recv, pair_send, pair_recv, up_send, up_recv,
           forward_send, up_forward_send, xy_send, xy_recv, core_send, core_recv):
    replica, tensor = lax.axis_index("replica"), lax.axis_index("tensor")
    z, y_hi = replica // 2, replica % 2
    y, x, core = y_hi * 2 + tensor // 8, (tensor // 2) % NX, tensor % 2
    mine, slot = block_of(x, y, core), exchanged(z)
    first, second = z < CUBE, z // CUBE == 1
    last, not_first = z >= HALF, z >= CUBE

    def column(k):
        return place(x, y, k, core)

    plane = [place((x + dx) % NX, (y + dy) % NY, z, core) for dx, dy in PLANE]
    partner = place(x, y, z, 1 - core)

    barrier = pltpu.get_barrier_semaphore()

    def signal(where):
        pl.semaphore_signal(barrier, inc=1, device_id=where, device_id_type=MESH)

    @pl.when(z < HALF)
    def _():
        for k in range(HALF, NZ):
            signal(column(k))

    @pl.when(first)
    def _():
        for k in range(CUBE, HALF):
            signal(column(k))
        for k in range(1, CUBE):
            signal(column((z + k) % CUBE))

    for where in plane:
        signal(where)
    signal(partner)

    my_up = up_ref.at[:, pl.ds(pl.multiple_of(tensor // 2 * LANES, LANES), LANES)]
    own_tile = pltpu.make_async_copy(down_ref, tiles.at[mine, slot], small_sem.at[0])
    own_up = pltpu.make_async_copy(my_up, pair_up.at[y_hi], small_sem.at[1])
    get_index = pltpu.make_async_copy(index_ref, index, small_sem.at[2])
    get_weight = pltpu.make_async_copy(weight_ref, weight, weight_sem)

    @pl.when(first)
    def _():
        own_tile.start()

    own_up.start()
    get_index.start()
    get_weight.start()

    def copy(source, target, send_sem, recv_sem, where):
        pltpu.make_async_remote_copy(src_ref=source, dst_ref=target, send_sem=send_sem, recv_sem=recv_sem,
                                     device_id=where, device_id_type=MESH).start()

    def send(ref, send_sem, recv_sem, where):
        copy(ref, ref, send_sem, recv_sem, where)

    def wait(ref, sem):
        pltpu.make_async_copy(ref, ref, sem).wait()

    def slots(w, start, size):
        return tiles.at[w, pl.ds(start, size)]

    def over_plane(g, start, size):
        for where in plane:
            send(slots(mine, start, size), xy_send, xy_recv.at[x, g], where)

    def exchange_ups(others):
        copy(my_up, pair_up.at[y_hi], pair_send, pair_recv, place(x, (y + 2) % NY, z, core))
        own_up.wait()
        wait(pair_up.at[1 - y_hi], pair_recv)
        for where in others:
            copy(pair_up, ups.at[slot], up_send, up_recv, where)

    @pl.when(first)
    def _():
        pl.semaphore_wait(barrier, CUBE - 1 + len(PLANE) + 1)
        others = [column((z + k) % CUBE) for k in range(1, CUBE)]
        for where in others:
            copy(down_ref, tiles.at[mine, slot], z_send, z_recv.at[0], where)
        exchange_ups(others)
        ups[slot] = pair_up[...]
        own_tile.wait()
        wait(slots(mine, 0, CUBE - 1), z_recv.at[0])
        over_plane(0, 0, CUBE)
        wait(slots(mine, CUBE, 2 * CUBE), z_recv.at[1])
        over_plane(1, CUBE, 2 * CUBE)
        for k in (CUBE, 3 * CUBE):
            send(slots(mine, 0, HALF), forward_send, z_recv.at[2], column(z + k))
        wait(slots(mine, 3 * CUBE, CUBE), z_recv.at[2])
        over_plane(2, 3 * CUBE, CUBE)
        send(slots(mine, HALF, HALF), forward_send, z_recv.at[1], column(z + 3 * CUBE))

    @pl.when(second)
    def _():
        pl.semaphore_wait(barrier, CUBE + len(PLANE) + 1)
        others = [column(k) for k in range(CUBE)]
        for where in others:
            copy(down_ref, tiles.at[mine, slot], z_send, z_recv.at[1], where)
        exchange_ups(others)

    @pl.when(last)
    def _():
        pl.semaphore_wait(barrier, HALF + len(PLANE) + 1)
        for k in range(CUBE):
            copy(down_ref, tiles.at[mine, slot], z_send, z_recv.at[1 + slot // (3 * CUBE)], column(k))
        for k in range(CUBE, HALF):
            copy(down_ref, tiles.at[mine, slot], z_send, z_recv.at[1], column(k))
        exchange_ups([column(k) for k in range(HALF)])

    @pl.when(not_first)
    def _():
        for g, start in ((1, HALF), (2, 0)):
            wait(slots(mine, start, HALF), z_recv.at[g])
            over_plane(g, start, HALF)

            @pl.when(second)
            def _():
                send(slots(mine, start, HALF), forward_send, z_recv.at[g], column(z + CUBE))

    def cut(a, count, start, size, which):
        return tiles.at[pl.ds(block_of(a, 0, which), count), pl.ds(start, size)]

    def arrived(a, own, g, start, size):
        wait(cut(a, NY - 1 if own else NY, start, size, core), xy_recv.at[a, g])

    columns = [((x + dx) % NX, dx == 0) for dx in (0, 1, 3, 2)]

    @pl.when(first)
    def _():
        for g, start, size in ((0, 0, CUBE), (1, CUBE, 2 * CUBE)):
            for a, own in columns:
                arrived(a, own, g, start, size)

    @pl.when(not_first)
    def _():
        for a, own in columns:
            arrived(a, own, 1, HALF, HALF)

    leading = jnp.where(first, 0, HALF)
    send(cut(0, NX * NY, leading, HALF, core), core_send.at[0], core_recv.at[NX], partner)

    @pl.when(first)
    def _():
        wait(ups.at[pl.ds(0, NZ - 1)], up_recv)
        send(ups.at[pl.ds(0, HALF)], up_forward_send, up_recv, column(z + CUBE))
        send(ups, up_forward_send, up_recv, column(z + 3 * CUBE))

    @pl.when(not_first)
    def _():
        wait(ups, up_recv)

    @pl.when(second)
    def _():
        send(ups, up_forward_send, up_recv, column(z + CUBE))

    get_index.wait()

    iota = lambda shape, dim: lax.broadcasted_iota(jnp.int32, shape, dim)
    k32 = iota((192, 32), 0) % 64
    owner = exchanged(k32 % 16) * 2 + k32 // 32
    holds = (index[...] == owner).astype(jnp.bfloat16)
    q = iota((32, 64), 1)
    spread = (iota((32, 64), 0) == exchanged(q // 4) * 2 + (q // 2) % 2).astype(jnp.bfloat16)
    k64, q64 = iota((192, 64), 0), iota((192, 64), 1)
    pick = jnp.dot(holds, spread, preferred_element_type=jnp.float32)
    pick = jnp.where(q64 % 2 == (k64 // 16) % 2, pick, 0.0)
    pick_high = jnp.where(k64 < 128, pick, 0.0).astype(jnp.bfloat16)
    pick_low = jnp.where(k64 < 128, 0.0, pick).astype(jnp.bfloat16)
    turned = (MERGE_SCALE * ups[...].reshape(64, LANES)).T
    high = turned.astype(jnp.bfloat16)
    low = (turned - high.astype(jnp.float32)).astype(jnp.bfloat16)
    nt = (((1,), (1,)), ((), ()))
    left[...] = (lax.dot_general(high, pick_high, nt, preferred_element_type=jnp.float32)
                 + lax.dot_general(low, pick_low, nt, preferred_element_type=jnp.float32)).astype(jnp.bfloat16)
    get_weight.wait()

    def merge(a, b_low, which):
        parts = []
        for c in range(4):
            parts.append(jnp.concatenate(
                [tiles[w, :, c * 2 + i, :]
                 for w in (block_of(a, b_low, which), block_of(a, b_low + 2, which)) for i in range(2)], axis=0))
        right = jnp.concatenate(parts, axis=1)
        right_high = right.astype(jnp.bfloat16)
        right_low = (right - right_high.astype(jnp.float32)).astype(jnp.bfloat16)
        right = jnp.concatenate([right_high, right_low, right_high], axis=0)
        update = jnp.dot(left[...], right, preferred_element_type=jnp.float32)
        at = pl.ds(pl.multiple_of(((b_low * NX + a) * 2 + which) * COLUMNS, COLUMNS), COLUMNS)
        out_ref[:, at] = (weight[:, at].astype(jnp.float32) + update).astype(jnp.bfloat16)

    def from_sibling(a):
        wait(cut(a, NY, 0, HALF, 1 - core), core_recv.at[a])
        for b in range(2):
            merge(a, b, 1 - core)

    for n, (a, own) in enumerate(columns):
        @pl.when(first)
        def _():
            arrived(a, own, 2, 3 * CUBE, CUBE)

        @pl.when(not_first)
        def _():
            arrived(a, own, 2, 0, HALF)

        send(cut(a, NY, HALF - leading, HALF, core), core_send.at[1], core_recv.at[a], partner)
        for b in range(2):
            merge(a, b, core)
        if n == 0:
            wait(cut(0, NX * NY, 0, HALF, 1 - core), core_recv.at[NX])
        else:
            from_sibling(columns[n - 1][0])
    from_sibling(columns[-1][0])

    wait(pair_up.at[0], pair_send)

    @pl.when(first)
    def _():
        wait(slots(mine, 0, CUBE - 1), z_send)
        wait(ups.at[pl.ds(0, CUBE - 1)], up_send)
        wait(tiles.at[pl.ds(0, 3), pl.ds(0, HALF)], forward_send)
        wait(slots(mine, 0, 12), up_forward_send)

    @pl.when(second)
    def _():
        wait(slots(mine, 0, CUBE), z_send)
        wait(ups.at[pl.ds(0, CUBE)], up_send)
        wait(tiles.at[mine], forward_send)
        wait(ups, up_forward_send)

    @pl.when(last)
    def _():
        wait(slots(mine, 0, HALF), z_send)
        wait(ups.at[pl.ds(0, HALF)], up_send)

    wait(tiles.at[pl.ds(0, 15)], xy_send)
    for k in range(2):
        wait(cut(0, NX * NY, 0, HALF, core), core_send.at[k])


def local(key_head_weight, down_factor_slots, adapter_up_factor, piece_slot_index):
    units, width = key_head_weight.shape[1:]
    tile = down_factor_slots.reshape(2, 4, LANES).transpose(1, 0, 2).reshape(8, LANES)
    dma = pltpu.SemaphoreType.DMA
    operands = (piece_slot_index.reshape(1, 32), tile, adapter_up_factor, key_head_weight.reshape(units, width))
    merged = pl.pallas_call(
        kernel,
        out_shape=jax.ShapeDtypeStruct((units, width), jnp.bfloat16),
        in_specs=[pl.BlockSpec(memory_space=pltpu.HBM)] * 4,
        out_specs=pl.BlockSpec(memory_space=pltpu.VMEM),
        scratch_shapes=[
            pltpu.VMEM((1, 32), jnp.int32),
            pltpu.VMEM((32, NZ, 8, LANES), jnp.float32),
            pltpu.VMEM((NZ, 2, 2, LANES), jnp.float32),
            pltpu.VMEM((2, 2, LANES), jnp.float32),
            pltpu.VMEM((units, width), jnp.bfloat16),
            pltpu.VMEM((units, 192), jnp.bfloat16),
            dma, dma((3,)), dma, dma((3,)), dma, dma, dma, dma, dma, dma,
            dma, dma((NX, 3)), dma((2,)), dma((NX + 1,)),
        ],
        compiler_params=pltpu.CompilerParams(
            collective_id=0, has_side_effects=True, vmem_limit_bytes=32 << 20),
        name="gather_and_merge",
    )(*[pltpu.with_memory_space_constraint(a, pltpu.HBM) for a in operands])
    return merged.reshape(1, units, width)


def solution(mesh):
    in_specs = (P("tensor", None, None), P("replica", None, "tensor"), P("replica", None), P())
    out_specs = P("tensor", None, None)
    return jax.shard_map(local, mesh=mesh, in_specs=in_specs, out_specs=out_specs, check_vma=False)
```

time: 48.6 us -> 40.1 us (0.83)
  the two profiles are of different devices: /device:TPU:1 before, /device:TPU:325 now
where the time goes in v2:
time: 40.1 us; the launch traced here: 40 us
  Pallas kernels  38.6 us (96%)
  local copies, waits for them, and re-layouts  1.32 us (3%)
    pallas_call x1, Pallas kernels, local(): pl.pallas_call(kernel, out_shape=jax.ShapeDtypeStruct((units, width), jnp...  38.6 us
    unnamed x1, local copies, waits for them, and re-layouts  1.32 us

profile of v2, /device:TPU:325, one launch (start us, length us, event | category | flops | bytes accessed | tf_op | source)
XLA Modules:
  0.0 40.0 jit_solution(2293045036714082220)
XLA Ops:
  0.0 38.6 %gather_and_merge.1 = bf16[128,8192]{1,0:T(8,128)(2,1)S(1)} custom-call(s32[1,32]{1,0:T(1,128)} %bitcast.11, f32[8,128]{1,0:T(8,128)} %bitcast.10, f32[2,1024]{1,0:T(2,128)} %up_ref.1, bf16[128,8192]{1,0:T(8,128)(2,1)} %bitcast.9), custom_call_target="tpu_custom_call" | custom-call | tf_op jit(solution)/shard_map/gather_and_merge/pallas_call | solution.py:277
  38.6 1.3 %copy.7 = bf16[1,128,8192]{2,1,0:T(8,128)(2,1)} copy(bf16[1,128,8192]{2,1,0:T(8,128)(2,1)S(1)} %bitcast.8) | data formatting | bytes 4194304

commit v3 on v2

--- a/solution.py
+++ b/solution.py
@@ -30,7 +30,7 @@
 
 def kernel(index_ref, down_ref, up_ref, weight_ref, out_ref, index, tiles, ups, pair_up, weight, left,
            weight_sem, small_sem, z_send, z_recv, pair_send, pair_recv, up_send, up_recv,
-           forward_send, up_forward_send, xy_send, xy_recv, core_send, core_recv):
+           up_late_recv, here, forward_send, up_forward_send, xy_send, xy_recv, core_send, core_recv):
     replica, tensor = lax.axis_index("replica"), lax.axis_index("tensor")
     z, y_hi = replica // 2, replica % 2
     y, x, core = y_hi * 2 + tensor // 8, (tensor // 2) % NX, tensor % 2
@@ -61,6 +61,18 @@
         for k in range(1, CUBE):
             signal(column((z + k) % CUBE))
 
+    @pl.when(second)
+    def _():
+        for k in range(1, CUBE):
+            signal(column(CUBE + (z + k) % CUBE))
+
+    late_others = [column(HALF + (z + k) % HALF) for k in range(1, HALF)]
+
+    @pl.when(last)
+    def _():
+        for where in late_others:
+            signal(where)
+
     for where in plane:
         signal(where)
     signal(partner)
@@ -71,10 +83,7 @@
     get_index = pltpu.make_async_copy(index_ref, index, small_sem.at[2])
     get_weight = pltpu.make_async_copy(weight_ref, weight, weight_sem)
 
-    @pl.when(first)
-    def _():
-        own_tile.start()
-
+    own_tile.start()
     own_up.start()
     get_index.start()
     get_weight.start()
@@ -96,12 +105,16 @@
         for where in plane:
             send(slots(mine, start, size), xy_send, xy_recv.at[x, g], where)
 
-    def exchange_ups(others):
+    def swap_ups():
         copy(my_up, pair_up.at[y_hi], pair_send, pair_recv, place(x, (y + 2) % NY, z, core))
+
+    def send_ups(others, recv_sem):
         own_up.wait()
         wait(pair_up.at[1 - y_hi], pair_recv)
         for where in others:
-            copy(pair_up, ups.at[slot], up_send, up_recv, where)
+            copy(pair_up, ups.at[slot], up_send, recv_sem, where)
+
+    early_ups, late_ups = ups.at[pl.ds(0, HALF)], ups.at[pl.ds(HALF, HALF)]
 
     @pl.when(first)
     def _():
@@ -109,81 +122,107 @@
         others = [column((z + k) % CUBE) for k in range(1, CUBE)]
         for where in others:
             copy(down_ref, tiles.at[mine, slot], z_send, z_recv.at[0], where)
-        exchange_ups(others)
+        swap_ups()
+        send_ups(others, up_recv)
         ups[slot] = pair_up[...]
         own_tile.wait()
         wait(slots(mine, 0, CUBE - 1), z_recv.at[0])
         over_plane(0, 0, CUBE)
-        wait(slots(mine, CUBE, 2 * CUBE), z_recv.at[1])
-        over_plane(1, CUBE, 2 * CUBE)
+        pl.semaphore_wait(here, 1)
+        send(slots(mine, 0, CUBE), forward_send, z_recv.at[0], column(z + CUBE))
+        wait(slots(mine, CUBE, CUBE), z_recv.at[1])
+        over_plane(1, CUBE, CUBE)
+        wait(slots(mine, HALF, CUBE), z_recv.at[2])
+        send(slots(mine, 0, HALF), forward_send, z_recv.at[0], column(z + 3 * CUBE))
+        over_plane(2, HALF, CUBE)
+        wait(slots(mine, 3 * CUBE, CUBE), z_recv.at[3])
+        over_plane(3, 3 * CUBE, CUBE)
+        wait(ups.at[pl.ds(0, HALF - 1)], up_recv)
         for k in (CUBE, 3 * CUBE):
-            send(slots(mine, 0, HALF), forward_send, z_recv.at[2], column(z + k))
-        wait(slots(mine, 3 * CUBE, CUBE), z_recv.at[2])
-        over_plane(2, 3 * CUBE, CUBE)
-        send(slots(mine, HALF, HALF), forward_send, z_recv.at[1], column(z + 3 * CUBE))
+            send(early_ups, up_forward_send, up_recv, column(z + k))
 
     @pl.when(second)
     def _():
-        pl.semaphore_wait(barrier, CUBE + len(PLANE) + 1)
-        others = [column(k) for k in range(CUBE)]
-        for where in others:
-            copy(down_ref, tiles.at[mine, slot], z_send, z_recv.at[1], where)
-        exchange_ups(others)
+        pl.semaphore_wait(barrier, HALF - 1 + len(PLANE) + 1)
+        pl.semaphore_signal(here, inc=1, device_id=column(z - CUBE), device_id_type=MESH)
+        for k in range(CUBE):
+            copy(down_ref, tiles.at[mine, slot], z_send, z_recv.at[1], column(k))
+        for k in range(1, CUBE):
+            copy(down_ref, tiles.at[mine, slot], z_send, z_recv.at[1], column(CUBE + (z + k) % CUBE))
+        swap_ups()
+        send_ups([column(k) for k in range(CUBE)], up_recv)
+        own_tile.wait()
+        wait(slots(mine, CUBE, CUBE - 1), z_recv.at[1])
+        over_plane(1, CUBE, CUBE)
+        wait(slots(mine, HALF, HALF), z_recv.at[2])
+        wait(slots(mine, 0, CUBE), z_recv.at[0])
+        send(slots(mine, 0, HALF), forward_send, z_recv.at[0], column(z + CUBE))
+        over_plane(2, HALF, HALF)
+        over_plane(0, 0, CUBE)
+        wait(early_ups, up_recv)
+        send(early_ups, up_forward_send, up_recv, column(z + CUBE))
 
     @pl.when(last)
     def _():
-        pl.semaphore_wait(barrier, HALF + len(PLANE) + 1)
+        pl.semaphore_wait(barrier, NZ - 1 + len(PLANE) + 1)
         for k in range(CUBE):
-            copy(down_ref, tiles.at[mine, slot], z_send, z_recv.at[1 + slot // (3 * CUBE)], column(k))
+            copy(down_ref, tiles.at[mine, slot], z_send, z_recv.at[2 + slot // (3 * CUBE)], column(k))
         for k in range(CUBE, HALF):
-            copy(down_ref, tiles.at[mine, slot], z_send, z_recv.at[1], column(k))
-        exchange_ups([column(k) for k in range(HALF)])
-
-    @pl.when(not_first)
-    def _():
-        for g, start in ((1, HALF), (2, 0)):
-            wait(slots(mine, start, HALF), z_recv.at[g])
-            over_plane(g, start, HALF)
-
+            copy(down_ref, tiles.at[mine, slot], z_send, z_recv.at[2], column(k))
+        swap_ups()
+        for where in late_others:
+            copy(down_ref, tiles.at[mine, slot], z_send, z_recv.at[2], where)
+        send_ups([column(k) for k in range(HALF)] + late_others, up_late_recv)
+        ups[slot] = pair_up[...]
+        own_tile.wait()
+        wait(slots(mine, HALF, HALF - 1), z_recv.at[2])
+        over_plane(2, HALF, HALF)
+        wait(slots(mine, 0, HALF), z_recv.at[0])
+        over_plane(0, 0, HALF)
+
+    def cut(a, count, start, size, which):
+        return tiles.at[pl.ds(block_of(a, 0, which), count), pl.ds(start, size)]
+
+    def arrived(a, own, g, start, size):
+        wait(cut(a, NY - 1 if own else NY, start, size, core), xy_recv.at[a, g])
+
+    columns = [((x + dx) % NX, dx == 0) for dx in (0, 1, 3, 2)]
+
+    def arrive(a, own, lead):
+        @pl.when(first)
+        def _():
+            for g in (0, 1) if lead else (2, 3):
+                arrived(a, own, g, 0, CUBE)
+
+        @pl.when(not_first)
+        def _():
+            if lead:
+                arrived(a, own, 2, 0, HALF)
+
+        if not lead:
             @pl.when(second)
             def _():
-                send(slots(mine, start, HALF), forward_send, z_recv.at[g], column(z + CUBE))
-
-    def cut(a, count, start, size, which):
-        return tiles.at[pl.ds(block_of(a, 0, which), count), pl.ds(start, size)]
-
-    def arrived(a, own, g, start, size):
-        wait(cut(a, NY - 1 if own else NY, start, size, core), xy_recv.at[a, g])
-
-    columns = [((x + dx) % NX, dx == 0) for dx in (0, 1, 3, 2)]
-
-    @pl.when(first)
-    def _():
-        for g, start, size in ((0, 0, CUBE), (1, CUBE, 2 * CUBE)):
-            for a, own in columns:
-                arrived(a, own, g, start, size)
-
-    @pl.when(not_first)
-    def _():
-        for a, own in columns:
-            arrived(a, own, 1, HALF, HALF)
+                for g in (1, 0):
+                    arrived(a, own, g, 0, CUBE)
+
+            @pl.when(last)
+            def _():
+                arrived(a, own, 0, 0, HALF)
+
+    for a, own in columns:
+        arrive(a, own, True)
 
     leading = jnp.where(first, 0, HALF)
     send(cut(0, NX * NY, leading, HALF, core), core_send.at[0], core_recv.at[NX], partner)
 
-    @pl.when(first)
-    def _():
-        wait(ups.at[pl.ds(0, NZ - 1)], up_recv)
-        send(ups.at[pl.ds(0, HALF)], up_forward_send, up_recv, column(z + CUBE))
-        send(ups, up_forward_send, up_recv, column(z + 3 * CUBE))
-
-    @pl.when(not_first)
-    def _():
-        wait(ups, up_recv)
-
-    @pl.when(second)
-    def _():
-        send(ups, up_forward_send, up_recv, column(z + CUBE))
+    @pl.when(z < HALF)
+    def _():
+        wait(late_ups, up_late_recv)
+
+    @pl.when(last)
+    def _():
+        wait(early_ups, up_recv)
+        wait(ups.at[pl.ds(HALF, HALF - 1)], up_late_recv)
 
     get_index.wait()
 
@@ -226,14 +265,7 @@
             merge(a, b, 1 - core)
 
     for n, (a, own) in enumerate(columns):
-        @pl.when(first)
-        def _():
-            arrived(a, own, 2, 3 * CUBE, CUBE)
-
-        @pl.when(not_first)
-        def _():
-            arrived(a, own, 2, 0, HALF)
-
+        arrive(a, own, False)
         send(cut(a, NY, HALF - leading, HALF, core), core_send.at[1], core_recv.at[a], partner)
         for b in range(2):
             merge(a, b, core)
@@ -249,20 +281,20 @@
     def _():
         wait(slots(mine, 0, CUBE - 1), z_send)
         wait(ups.at[pl.ds(0, CUBE - 1)], up_send)
-        wait(tiles.at[pl.ds(0, 3), pl.ds(0, HALF)], forward_send)
-        wait(slots(mine, 0, 12), up_forward_send)
+        wait(slots(mine, 0, 3 * CUBE), forward_send)
+        wait(ups, up_forward_send)
 
     @pl.when(second)
     def _():
-        wait(slots(mine, 0, CUBE), z_send)
+        wait(slots(mine, 0, HALF - 1), z_send)
         wait(ups.at[pl.ds(0, CUBE)], up_send)
-        wait(tiles.at[mine], forward_send)
-        wait(ups, up_forward_send)
+        wait(slots(mine, 0, HALF), forward_send)
+        wait(early_ups, up_forward_send)
 
     @pl.when(last)
     def _():
-        wait(slots(mine, 0, HALF), z_send)
-        wait(ups.at[pl.ds(0, HALF)], up_send)
+        wait(slots(mine, 0, NZ - 1), z_send)
+        wait(ups.at[pl.ds(0, NZ - 1)], up_send)
 
     wait(tiles.at[pl.ds(0, 15)], xy_send)
     for k in range(2):
@@ -286,8 +318,8 @@
             pltpu.VMEM((2, 2, LANES), jnp.float32),
             pltpu.VMEM((units, width), jnp.bfloat16),
             pltpu.VMEM((units, 192), jnp.bfloat16),
-            dma, dma((3,)), dma, dma((3,)), dma, dma, dma, dma, dma, dma,
-            dma, dma((NX, 3)), dma((2,)), dma((NX + 1,)),
+            dma, dma((3,)), dma, dma((4,)), dma, dma, dma, dma,
+            dma, pltpu.SemaphoreType.REGULAR, dma, dma, dma, dma((NX, 4)), dma((2,)), dma((NX + 1,)),
         ],
         compiler_params=pltpu.CompilerParams(
             collective_id=0, has_side_effects=True, vmem_limit_bytes=32 << 20),

time: 40.1 us -> 34.3 us (0.86)
  the two profiles are of different devices: /device:TPU:325 before, /device:TPU:1 now
where the time goes in v3:
time: 34.3 us; the launch traced here: 34.2 us
  Pallas kernels  32.8 us (96%)
  local copies, waits for them, and re-layouts  1.32 us (4%)
    pallas_call x1, Pallas kernels, local(): pl.pallas_call(kernel, out_shape=jax.ShapeDtypeStruct((units, width), jnp...  32.8 us
    unnamed x1, local copies, waits for them, and re-layouts  1.32 us

profile of v3, /device:TPU:1, one launch (start us, length us, event | category | flops | bytes accessed | tf_op | source)
XLA Modules:
  0.0 34.2 jit_solution(11216165288569544539)
XLA Ops:
  0.0 32.8 %gather_and_merge.1 = bf16[128,8192]{1,0:T(8,128)(2,1)S(1)} custom-call(s32[1,32]{1,0:T(1,128)} %bitcast.11, f32[8,128]{1,0:T(8,128)} %bitcast.10, f32[2,1024]{1,0:T(2,128)} %up_ref.1, bf16[128,8192]{1,0:T(8,128)(2,1)} %bitcast.9), custom_call_target="tpu_custom_call" | custom-call | tf_op jit(solution)/shard_map/gather_and_merge/pallas_call | solution.py:309
  32.9 1.3 %copy.7 = bf16[1,128,8192]{2,1,0:T(8,128)(2,1)} copy(bf16[1,128,8192]{2,1,0:T(8,128)(2,1)S(1)} %bitcast.8) | data formatting | bytes 4194304

commit v4 on v3

--- a/solution.py
+++ b/solution.py
@@ -36,7 +36,7 @@
     y, x, core = y_hi * 2 + tensor // 8, (tensor // 2) % NX, tensor % 2
     mine, slot = block_of(x, y, core), exchanged(z)
     first, second = z < CUBE, z // CUBE == 1
-    last, not_first = z >= HALF, z >= CUBE
+    last = z >= HALF
 
     def column(k):
         return place(x, y, k, core)
@@ -49,33 +49,31 @@
     def signal(where):
         pl.semaphore_signal(barrier, inc=1, device_id=where, device_id_type=MESH)
 
-    @pl.when(z < HALF)
-    def _():
-        for k in range(HALF, NZ):
-            signal(column(k))
-
-    @pl.when(first)
-    def _():
-        for k in range(CUBE, HALF):
-            signal(column(k))
-        for k in range(1, CUBE):
-            signal(column((z + k) % CUBE))
-
-    @pl.when(second)
-    def _():
-        for k in range(1, CUBE):
-            signal(column(CUBE + (z + k) % CUBE))
-
-    late_others = [column(HALF + (z + k) % HALF) for k in range(1, HALF)]
+    late_others = [column(HALF + (z + k) % HALF) for k in (4, 5, 3, 6, 2, 7, 1)]
 
     @pl.when(last)
     def _():
         for where in late_others:
             signal(where)
+
+    @pl.when(z < HALF)
+    def _():
+        for k in range(1, CUBE):
+            signal(column(z // CUBE * CUBE + (z + k) % CUBE))
 
     for where in plane:
         signal(where)
     signal(partner)
+
+    @pl.when(first)
+    def _():
+        for k in range(CUBE, HALF):
+            signal(column(k))
+
+    @pl.when(z < HALF)
+    def _():
+        for k in range(HALF, NZ):
+            signal(column(k))
 
     my_up = up_ref.at[:, pl.ds(pl.multiple_of(tensor // 2 * LANES, LANES), LANES)]
     own_tile = pltpu.make_async_copy(down_ref, tiles.at[mine, slot], small_sem.at[0])
@@ -105,6 +103,8 @@
         for where in plane:
             send(slots(mine, start, size), xy_send, xy_recv.at[x, g], where)
 
+    own_tile.wait()
+
     def swap_ups():
         copy(my_up, pair_up.at[y_hi], pair_send, pair_recv, place(x, (y + 2) % NY, z, core))
 
@@ -121,11 +121,10 @@
         pl.semaphore_wait(barrier, CUBE - 1 + len(PLANE) + 1)
         others = [column((z + k) % CUBE) for k in range(1, CUBE)]
         for where in others:
-            copy(down_ref, tiles.at[mine, slot], z_send, z_recv.at[0], where)
+            send(tiles.at[mine, slot], z_send, z_recv.at[0], where)
         swap_ups()
         send_ups(others, up_recv)
         ups[slot] = pair_up[...]
-        own_tile.wait()
         wait(slots(mine, 0, CUBE - 1), z_recv.at[0])
         over_plane(0, 0, CUBE)
         pl.semaphore_wait(here, 1)
@@ -146,35 +145,33 @@
         pl.semaphore_wait(barrier, HALF - 1 + len(PLANE) + 1)
         pl.semaphore_signal(here, inc=1, device_id=column(z - CUBE), device_id_type=MESH)
         for k in range(CUBE):
-            copy(down_ref, tiles.at[mine, slot], z_send, z_recv.at[1], column(k))
+            send(tiles.at[mine, slot], z_send, z_recv.at[1], column(k))
         for k in range(1, CUBE):
-            copy(down_ref, tiles.at[mine, slot], z_send, z_recv.at[1], column(CUBE + (z + k) % CUBE))
+            send(tiles.at[mine, slot], z_send, z_recv.at[1], column(CUBE + (z + k) % CUBE))
         swap_ups()
         send_ups([column(k) for k in range(CUBE)], up_recv)
-        own_tile.wait()
         wait(slots(mine, CUBE, CUBE - 1), z_recv.at[1])
         over_plane(1, CUBE, CUBE)
-        wait(slots(mine, HALF, HALF), z_recv.at[2])
+        wait(slots(mine, 3 * CUBE, CUBE), z_recv.at[3])
         wait(slots(mine, 0, CUBE), z_recv.at[0])
         send(slots(mine, 0, HALF), forward_send, z_recv.at[0], column(z + CUBE))
-        over_plane(2, HALF, HALF)
         over_plane(0, 0, CUBE)
+        over_plane(3, 3 * CUBE, CUBE)
+        wait(slots(mine, HALF, CUBE), z_recv.at[2])
+        over_plane(2, HALF, CUBE)
         wait(early_ups, up_recv)
         send(early_ups, up_forward_send, up_recv, column(z + CUBE))
 
     @pl.when(last)
     def _():
         pl.semaphore_wait(barrier, NZ - 1 + len(PLANE) + 1)
-        for k in range(CUBE):
-            copy(down_ref, tiles.at[mine, slot], z_send, z_recv.at[2 + slot // (3 * CUBE)], column(k))
-        for k in range(CUBE, HALF):
-            copy(down_ref, tiles.at[mine, slot], z_send, z_recv.at[2], column(k))
         swap_ups()
+        for k in range(HALF):
+            send(tiles.at[mine, slot], z_send, z_recv.at[2 + slot // (3 * CUBE)], column(k))
         for where in late_others:
-            copy(down_ref, tiles.at[mine, slot], z_send, z_recv.at[2], where)
+            send(tiles.at[mine, slot], z_send, z_recv.at[2], where)
         send_ups([column(k) for k in range(HALF)] + late_others, up_late_recv)
         ups[slot] = pair_up[...]
-        own_tile.wait()
         wait(slots(mine, HALF, HALF - 1), z_recv.at[2])
         over_plane(2, HALF, HALF)
         wait(slots(mine, 0, HALF), z_recv.at[0])
@@ -189,30 +186,19 @@
     columns = [((x + dx) % NX, dx == 0) for dx in (0, 1, 3, 2)]
 
     def arrive(a, own, lead):
-        @pl.when(first)
+        @pl.when(z < HALF)
         def _():
             for g in (0, 1) if lead else (2, 3):
                 arrived(a, own, g, 0, CUBE)
 
-        @pl.when(not_first)
+        @pl.when(last)
         def _():
-            if lead:
-                arrived(a, own, 2, 0, HALF)
-
-        if not lead:
-            @pl.when(second)
-            def _():
-                for g in (1, 0):
-                    arrived(a, own, g, 0, CUBE)
-
-            @pl.when(last)
-            def _():
-                arrived(a, own, 0, 0, HALF)
+            arrived(a, own, 2 if lead else 0, 0, HALF)
 
     for a, own in columns:
         arrive(a, own, True)
 
-    leading = jnp.where(first, 0, HALF)
+    leading = jnp.where(last, HALF, 0)
     send(cut(0, NX * NY, leading, HALF, core), core_send.at[0], core_recv.at[NX], partner)
 
     @pl.when(z < HALF)
@@ -264,16 +250,33 @@
         for b in range(2):
             merge(a, b, 1 - core)
 
-    for n, (a, own) in enumerate(columns):
+    def hand_over(n):
+        a, own = columns[n]
         arrive(a, own, False)
         send(cut(a, NY, HALF - leading, HALF, core), core_send.at[1], core_recv.at[a], partner)
+
+    def merge_own(n):
         for b in range(2):
-            merge(a, b, core)
+            merge(columns[n][0], b, core)
+
+    def merge_other(n):
         if n == 0:
             wait(cut(0, NX * NY, 0, HALF, 1 - core), core_recv.at[NX])
-        else:
-            from_sibling(columns[n - 1][0])
-    from_sibling(columns[-1][0])
+        wait(cut(columns[n][0], NY, 0, HALF, 1 - core), core_recv.at[columns[n][0]])
+        for b in range(2):
+            merge(columns[n][0], b, 1 - core)
+
+    for n in range(NX):
+        hand_over(n)
+
+    merge_own(0)
+    merge_own(1)
+    merge_own(2)
+    merge_own(3)
+    merge_other(0)
+    merge_other(1)
+    merge_other(2)
+    merge_other(3)
 
     wait(pair_up.at[0], pair_send)
 

time: 34.3 us -> 33.6 us (0.980)
  Pallas kernels: 32.8 us -> 32.2 us
    pallas_call x1, Pallas kernels: 32.8 us -> 32.2 us  [local(): pl.pallas_call(kernel, out_shape=jax.ShapeDtypeStruct((units, width), jnp...]
where the time goes in v4:
time: 33.6 us; the launch traced here: 33.5 us
  Pallas kernels  32.2 us (96%)
  local copies, waits for them, and re-layouts  1.32 us (4%)
    pallas_call x1, Pallas kernels, local(): pl.pallas_call(kernel, out_shape=jax.ShapeDtypeStruct((units, width), jnp...  32.2 us
    unnamed x1, local copies, waits for them, and re-layouts  1.32 us

profile of v4, /device:TPU:1, one launch (start us, length us, event | category | flops | bytes accessed | tf_op | source)
XLA Modules:
  0.0 33.5 jit_solution(4253642151468532830)
XLA Ops:
  0.0 32.2 %gather_and_merge.1 = bf16[128,8192]{1,0:T(8,128)(2,1)S(1)} custom-call(s32[1,32]{1,0:T(1,128)} %bitcast.11, f32[8,128]{1,0:T(8,128)} %bitcast.10, f32[2,1024]{1,0:T(2,128)} %up_ref.1, bf16[128,8192]{1,0:T(8,128)(2,1)} %bitcast.9), custom_call_target="tpu_custom_call" | custom-call | tf_op jit(solution)/shard_map/gather_and_merge/pallas_call | solution.py:312
  32.2 1.3 %copy.7 = bf16[1,128,8192]{2,1,0:T(8,128)(2,1)} copy(bf16[1,128,8192]{2,1,0:T(8,128)(2,1)S(1)} %bitcast.8) | data formatting | bytes 4194304

commit v5 on v4

--- a/solution.py
+++ b/solution.py
@@ -12,8 +12,8 @@
 HALF = 8
 LANES = 128
 COLUMNS = 512
-PLANE = [(2, 2), (2, 1), (2, 3), (1, 2), (3, 2), (1, 1), (1, 3), (3, 1), (3, 3),
-         (2, 0), (0, 2), (1, 0), (3, 0), (0, 1), (0, 3)]
+PLANE = [(2, 2), (1, 2), (2, 1), (1, 1), (2, 0), (0, 2), (1, 0), (0, 1),
+         (2, 3), (3, 2), (1, 3), (3, 1), (3, 3), (3, 0), (0, 3)]
 
 
 def place(x, y, z, core):
@@ -30,7 +30,7 @@
 
 def kernel(index_ref, down_ref, up_ref, weight_ref, out_ref, index, tiles, ups, pair_up, weight, left,
            weight_sem, small_sem, z_send, z_recv, pair_send, pair_recv, up_send, up_recv,
-           up_late_recv, here, forward_send, up_forward_send, xy_send, xy_recv, core_send, core_recv):
+           up_late_recv, here, forward_send, up_forward_send, xy_send, xy_recv, turn_recv, core_send, core_recv):
     replica, tensor = lax.axis_index("replica"), lax.axis_index("tensor")
     z, y_hi = replica // 2, replica % 2
     y, x, core = y_hi * 2 + tensor // 8, (tensor // 2) % NX, tensor % 2
@@ -104,6 +104,26 @@
             send(slots(mine, start, size), xy_send, xy_recv.at[x, g], where)
 
     own_tile.wait()
+
+    turns = (1, 2, 3)
+    across = [(x + d) % NX for d in turns]
+    along = [(y + d) % NY for d in turns]
+    x_others = [place(a, y, z, core) for a in across]
+    y_others = [place(x, b, z, core) for b in along]
+
+    def spread(g, start):
+        for where in x_others:
+            send(slots(mine, start, CUBE), xy_send, turn_recv.at[x] if g == 1 else xy_recv.at[x, g], where)
+        for where in y_others:
+            send(slots(mine, start, CUBE), xy_send, turn_recv.at[NX + y] if g == 2 else xy_recv.at[x, g], where)
+
+    def pass_on(g, start):
+        for n in range(3):
+            a, b = (across[n], y) if g == 1 else (x, along[n])
+            w = block_of(a, b, core)
+            wait(slots(w, start, CUBE), turn_recv.at[across[n] if g == 1 else NX + along[n]])
+            for where in y_others if g == 1 else x_others:
+                send(slots(w, start, CUBE), xy_send, xy_recv.at[a, g], where)
 
     def swap_ups():
         copy(my_up, pair_up.at[y_hi], pair_send, pair_recv, place(x, (y + 2) % NY, z, core))
@@ -130,12 +150,14 @@
         pl.semaphore_wait(here, 1)
         send(slots(mine, 0, CUBE), forward_send, z_recv.at[0], column(z + CUBE))
         wait(slots(mine, CUBE, CUBE), z_recv.at[1])
-        over_plane(1, CUBE, CUBE)
+        spread(1, CUBE)
         wait(slots(mine, HALF, CUBE), z_recv.at[2])
         send(slots(mine, 0, HALF), forward_send, z_recv.at[0], column(z + 3 * CUBE))
-        over_plane(2, HALF, CUBE)
+        spread(2, HALF)
+        pass_on(1, CUBE)
         wait(slots(mine, 3 * CUBE, CUBE), z_recv.at[3])
         over_plane(3, 3 * CUBE, CUBE)
+        pass_on(2, HALF)
         wait(ups.at[pl.ds(0, HALF - 1)], up_recv)
         for k in (CUBE, 3 * CUBE):
             send(early_ups, up_forward_send, up_recv, column(z + k))
@@ -186,7 +208,17 @@
     columns = [((x + dx) % NX, dx == 0) for dx in (0, 1, 3, 2)]
 
     def arrive(a, own, lead):
-        @pl.when(z < HALF)
+        @pl.when(first)
+        def _():
+            if lead:
+                arrived(a, own, 0, 0, CUBE)
+                arrived(a, True, 1, 0, CUBE)
+            else:
+                if not own:
+                    arrived(a, False, 2, 0, CUBE)
+                arrived(a, own, 3, 0, CUBE)
+
+        @pl.when(second)
         def _():
             for g in (0, 1) if lead else (2, 3):
                 arrived(a, own, g, 0, CUBE)
@@ -322,7 +354,7 @@
             pltpu.VMEM((units, width), jnp.bfloat16),
             pltpu.VMEM((units, 192), jnp.bfloat16),
             dma, dma((3,)), dma, dma((4,)), dma, dma, dma, dma,
-            dma, pltpu.SemaphoreType.REGULAR, dma, dma, dma, dma((NX, 4)), dma((2,)), dma((NX + 1,)),
+            dma, pltpu.SemaphoreType.REGULAR, dma, dma, dma, dma((NX, 4)), dma((NX + NY,)), dma((2,)), dma((NX + 1,)),
         ],
         compiler_params=pltpu.CompilerParams(
             collective_id=0, has_side_effects=True, vmem_limit_bytes=32 << 20),

time: 33.6 us -> 33.4 us (level)
  no operation moved by 1% of the time
where the time goes in v5:
time: 33.4 us; the launch traced here: 33.3 us
  Pallas kernels  32 us (96%)
  local copies, waits for them, and re-layouts  1.32 us (4%)
    pallas_call x1, Pallas kernels, local(): pl.pallas_call(kernel, out_shape=jax.ShapeDtypeStruct((units, width), jnp...  32 us
    unnamed x1, local copies, waits for them, and re-layouts  1.32 us

profile of v5, /device:TPU:1, one launch (start us, length us, event | category | flops | bytes accessed | tf_op | source)
XLA Modules:
  0.0 33.3 jit_solution(11781139207392150838)
XLA Ops:
  0.0 32.0 %gather_and_merge.1 = bf16[128,8192]{1,0:T(8,128)(2,1)S(1)} custom-call(s32[1,32]{1,0:T(1,128)} %bitcast.11, f32[8,128]{1,0:T(8,128)} %bitcast.10, f32[2,1024]{1,0:T(2,128)} %up_ref.1, bf16[128,8192]{1,0:T(8,128)(2,1)} %bitcast.9), custom_call_target="tpu_custom_call" | custom-call | tf_op jit(solution)/shard_map/gather_and_merge/pallas_call | solution.py:344
  32.0 1.3 %copy.7 = bf16[1,128,8192]{2,1,0:T(8,128)(2,1)} copy(bf16[1,128,8192]{2,1,0:T(8,128)(2,1)S(1)} %bitcast.8) | data formatting | bytes 4194304

commit v6 on v4

--- a/solution.py
+++ b/solution.py
@@ -132,8 +132,8 @@
         wait(slots(mine, CUBE, CUBE), z_recv.at[1])
         over_plane(1, CUBE, CUBE)
         wait(slots(mine, HALF, CUBE), z_recv.at[2])
+        over_plane(2, HALF, CUBE)
         send(slots(mine, 0, HALF), forward_send, z_recv.at[0], column(z + 3 * CUBE))
-        over_plane(2, HALF, CUBE)
         wait(slots(mine, 3 * CUBE, CUBE), z_recv.at[3])
         over_plane(3, 3 * CUBE, CUBE)
         wait(ups.at[pl.ds(0, HALF - 1)], up_recv)

time: 33.6 us -> 33.6 us (level)
  no operation moved by 1% of the time
where the time goes in v6:
time: 33.6 us; the launch traced here: 33.5 us
  Pallas kernels  32.2 us (96%)
  local copies, waits for them, and re-layouts  1.32 us (4%)
    pallas_call x1, Pallas kernels, local(): pl.pallas_call(kernel, out_shape=jax.ShapeDtypeStruct((units, width), jnp...  32.2 us
    unnamed x1, local copies, waits for them, and re-layouts  1.32 us

profile of v6, /device:TPU:1, one launch (start us, length us, event | category | flops | bytes accessed | tf_op | source)
XLA Modules:
  0.0 33.5 jit_solution(6551347659657460898)
XLA Ops:
  0.0 32.2 %gather_and_merge.1 = bf16[128,8192]{1,0:T(8,128)(2,1)S(1)} custom-call(s32[1,32]{1,0:T(1,128)} %bitcast.11, f32[8,128]{1,0:T(8,128)} %bitcast.10, f32[2,1024]{1,0:T(2,128)} %up_ref.1, bf16[128,8192]{1,0:T(8,128)(2,1)} %bitcast.9), custom_call_target="tpu_custom_call" | custom-call | tf_op jit(solution)/shard_map/gather_and_merge/pallas_call | solution.py:312
  32.2 1.3 %copy.7 = bf16[1,128,8192]{2,1,0:T(8,128)(2,1)} copy(bf16[1,128,8192]{2,1,0:T(8,128)(2,1)S(1)} %bitcast.8) | data formatting | bytes 4194304
